TPU v7x, 256 devices: a whole 4x4x8 slice. The times are simulated.
256 devices in a mesh: chan: 64 (over z, y, core), row: 4 (over x).
Axes of the slice: x: 4, y: 4, z: 8, core: 2. Of those that a mesh axis runs over, the one named last changes fastest.
Arguments:
- generator: float32 [64, 1280, 1280], P('chan', 'row'), as said below
- hamiltonian: float32 [64, 1280, 1280], P('chan', 'row'), as said below
- recoupling: float32 [64, 1280, 1280], P('chan')
- channel_size: int32 [64], P('chan'), may hold values from 128 to 1280, as said below
- hole_first: int32 [64, 1280], P('chan'), may hold values 0 or 1
- hole_second: int32 [64, 1280], P('chan'), may hold values 0 or 1
Outputs:
- derivative: float32 [64, 1280, 1280], P('chan', 'row')
Inputs may be any that keep to these rules, and one draw needn't show every extreme that they name: generator is antisymmetric and hamiltonian symmetric in every channel block. hamiltonian is symmetric in every channel block. `channel_size`: some channel has exactly 1280 states.
All inputs are finite; a program needn't handle non-finite values. No bound on the sum of `hole_first` or of `hole_second` on one device may be relied on, other than what follows from the above.
Results may differ from a plain program's by a relative error of at most 0.000076.
Values sent between devices are 32-bit elements; how exact they have to be, the bound alone decides.
No kernel may reach another device: no remote copies, remote signals or barrier semaphores. Data moves between devices by JAX's collectives and lax.ppermute only.
A program may use at most 128 MiB of HBM per device.

v0:
```python
import jax
import jax.numpy as jnp
from jax import lax
from jax.sharding import PartitionSpec as P


def batched(left, right):
    return jnp.einsum("cij,cjk->cik", left, right, precision=lax.Precision.HIGHEST)


def shards(generator, hamiltonian, recoupling, channel_size, hole_first, hole_second):
    local_count = generator.shape[0]
    row_count = generator.shape[1]
    block_order = generator.shape[2]
    chan_count = lax.axis_size("chan")
    row_index = lax.axis_index("row")
    positions = jnp.arange(block_order, dtype=jnp.int32)
    inside = (positions[None, :] < channel_size[:, None]).astype(jnp.float32)
    row_inside = lax.dynamic_slice_in_dim(inside, row_index * row_count, row_count, 1)
    block_mask = row_inside[:, :, None] * inside[:, None, :]
    gen_live = generator * block_mask
    ham_live = hamiltonian * block_mask
    weight_pp = (1 - hole_first - hole_second).astype(jnp.float32)
    weight_ph = (hole_first - hole_second).astype(jnp.float32)
    piece_shape = (local_count, row_count, chan_count, block_order // chan_count)
    gen_moved, ham_moved = (
        lax.all_to_all(
            gen_live.reshape(piece_shape), "chan", split_axis=2, concat_axis=2, tiled=True
        ),
        lax.all_to_all(
            ham_live.reshape(piece_shape), "chan", split_axis=2, concat_axis=2, tiled=True
        ),
    )
    gen_bar = batched(gen_moved.reshape(generator.shape), recoupling)
    ham_bar = batched(ham_moved.reshape(generator.shape), recoupling)
    pieces = (
        lax.all_gather(gen_bar, "row", axis=1, tiled=True),
        lax.all_gather(ham_bar, "row", axis=1, tiled=True),
    )
    factor = weight_ph[:, None, :]
    gen_cols = gen_bar * factor
    ham_cols = ham_bar * factor
    ph_term = batched(gen_cols, pieces[1]) - batched(ham_cols, pieces[0])
    turned = jnp.einsum("cij,ckj->cik", ph_term, recoupling, precision=lax.Precision.HIGHEST)
    back_moved = lax.all_to_all(
        turned.reshape(piece_shape), "chan", split_axis=2, concat_axis=2, tiled=True
    )
    ph_back = back_moved.reshape(generator.shape)
    pieces = (
        lax.all_gather(gen_live, "row", axis=1, tiled=True),
        lax.all_gather(ham_live, "row", axis=1, tiled=True),
    )
    factor = weight_pp[:, None, :]
    gen_cols = gen_live * factor
    ham_cols = ham_live * factor
    ladder = batched(gen_cols, pieces[1]) - batched(ham_cols, pieces[0])
    return (ladder + ph_back) * block_mask


def solution(mesh):
    in_specs = (
        P("chan", "row", None),
        P("chan", "row", None),
        P("chan", None, None),
        P("chan"),
        P("chan", None),
        P("chan", None),
    )
    out_specs = P("chan", "row", None)
    return jax.shard_map(shards, mesh=mesh, in_specs=in_specs, out_specs=out_specs, check_vma=False)
```

profile of v0, /device:TPU:1, one launch (start us, length us, event | category | flops | bytes accessed | tf_op | source)
XLA Modules:
  0.0 404.9 jit_solution(18243573594442668754)
XLA Ops:
  7.2 2.2 multiply_multiply_fusion.1
  9.5 3.6 copy.20
  13.0 60.2 %all_to_all.15 = f32[1,320,64,20]{1,0,3,2:T(1,128)} all-to-all(f32[1,320,64,20]{1,0,3,2:T(1,128)} %bitcast.47), channel_id=1, replica_groups=mesh['chan'=64,'row'=4] {'chan'}, dimensions={2} | all-to-all | bytes 3276800 | tf_op jit(solution)/shard_map/all_to_all | solution.py:30
  73.2 7.7 %reduce.4 = f32[320,64,20]{0,2,1:T(8,128)} reduce(f32[1,320,64,20]{1,0,3,2:T(1,128)} %all_to_all.15, f32[]{:T(128)} %constant.18), dimensions={0}, to_apply=%all_to_all.10.reduce_sub_computation | reduce | bytes 3276804 | tf_op jit(solution)/shard_map/all_to_all | solution.py:30
  81.0 2.9 reshape.159
  83.8 11.5 %fusion = f32[320,1280]{1,0:T(8,128)} fusion(f32[320,1280]{0,1:T(8,128)} %reshape.159, f32[1,1280,1280]{2,1,0:T(8,128)} %param.8), kind=kOutput, calls=%fused_computation | convolution fusion | flops 6291456000 | bytes 9830400 | tf_op jit(solution)/shard_map/cij,cjk->cik/dot_general | solution.py:8
  95.3 0.0 all-gather.11.cloned.1.call-update
  95.3 0.0 all-gather.13.cloned.1.call-start
  95.4 3.2 copy.19
  98.6 54.1 %all_to_all.16 = f32[1,320,64,20]{1,0,3,2:T(1,128)S(1)} all-to-all(f32[1,320,64,20]{1,0,3,2:T(1,128)} %bitcast.48), channel_id=1, replica_groups=mesh['chan'=64,'row'=4] {'chan'}, dimensions={2} | all-to-all | bytes 3276800 | tf_op jit(solution)/shard_map/all_to_all | solution.py:27
  152.6 7.0 %reduce.2 = f32[320,64,20]{0,2,1:T(8,128)} reduce(f32[1,320,64,20]{1,0,3,2:T(1,128)S(1)} %all_to_all.16, f32[]{:T(128)} %constant.18), dimensions={0}, to_apply=%all_to_all.9.reduce_sub_computation | reduce | bytes 3276804 | tf_op jit(solution)/shard_map/all_to_all | solution.py:27
  159.6 2.0 reshape.156
  161.6 10.9 %fusion.2 = f32[320,1280]{1,0:T(8,128)} fusion(f32[320,1280]{0,1:T(8,128)S(1)} %reshape.156, f32[1,1280,1280]{2,1,0:T(8,128)} %param.8), kind=kOutput, calls=%fused_computation.2 | convolution fusion | flops 6291456000 | bytes 9830400 | tf_op jit(solution)/shard_map/cij,cjk->cik/dot_general | solution.py:8
  172.5 0.0 all-gather.9.cloned.1.call-start
  172.5 0.7 all-gather.9.cloned.1.call-update
  173.2 0.0 all-gather.7.cloned.1.call-start
  173.3 0.5 all-gather.7.cloned.1.call-update
  173.8 8.4 %dot_general.37 = f32[64,20,1280]{2,1,0:T(8,128)} reshape(f32[1,1280,1280]{2,1,0:T(8,128)} %param.8) | data formatting | bytes 13107200 | tf_op jit(solution)/shard_map/cij,ckj->cik/dot_general | solution.py:44
  182.3 0.0 all-gather.11.cloned.1.call-done
  182.4 11.7 %fusion.26 = f32[320,1280]{1,0:T(8,128)} fusion(f32[1280,1280]{1,0:T(8,128)} %all-gather.11.cloned.1.call-done, f32[320,1280]{1,0:T(8,128)S(1)} %copy-done.4, f32[1280]{0:T(1024)S(1)} %get-tuple-element.6), kind=kOutput, calls=%fused_computation.21 | convolution fusion | flops 6291865600 | bytes 9835520 | tf_op jit(solution)/shard_map/cij,cjk->cik/dot_general | solution.py:8
  194.0 46.6 %all-gather.13.cloned.1.call-done = f32[1280,1280]{1,0:T(8,128)} async-done(((f32[320,1280]{1,0:T(8,128)}), f32[1280,1280]{1,0:T(8,128)}) %all-gather.13.cloned.1.call-update) | async-done | bytes 6553616 | tf_op jit(solution)/shard_map/all_gather | solution.py:37
  240.6 10.5 %fusion.19 = f32[320,1280,1]{1,0,2:T(8,128)S(1)} fusion(f32[320,1280]{1,0:T(8,128)} %fusion.26, f32[1280,1280]{1,0:T(8,128)} %all-gather.13.cloned.1.call-done, f32[320,1280]{1,0:T(8,128)S(1)} %copy-done.3, f32[1280]{0:T(1024)S(1)} %get-tuple-element.6), kind=kOutput, calls=%fused_computation.14 | convolution fusion | flops 6292275200 | bytes 11473920 | tf_op jit(solution)/shard_map/cij,cjk->cik/dot_general | solution.py:8
  251.2 11.5 %fusion.30 = f32[1,320,64,20]{1,2,3,0:T(8,128)S(1)} fusion(f32[320,1280,1]{1,0,2:T(8,128)S(1)} %fusion.19, f32[64,20,1280]{2,1,0:T(8,128)S(1)} %copy-done), kind=kOutput, calls=%fused_computation.25 | convolution fusion | flops 6291456000 | bytes 9830400 | tf_op jit(solution)/shard_map/cij,ckj->cik/dot_general | solution.py:44
  262.7 3.3 copy.22
  266.0 11.0 %all-to-all-start.2 = ((f32[1,320,64,20]{1,0,3,2:T(1,128)}), f32[1,320,64,20]{1,0,3,2:T(1,128)}, u32[]{:S(2)}, u32[]{:S(2)}) async-start(f32[1,320,64,20]{1,0,3,2:T(1,128)} %copy.22), calls=%async_computation.2 | async-start | bytes 3932160 | tf_op jit(solution)/shard_map/all_to_all | solution.py:45
  277.0 36.6 %all-gather.9.cloned.1.call-done = f32[1,1280,1280]{2,1,0:T(8,128)} async-done(((f32[1,320,1280]{2,1,0:T(8,128)}), f32[1,1280,1280]{2,1,0:T(8,128)}) %all-gather.9.cloned.1.call-update) | async-done | bytes 6553616 | tf_op jit(solution)/shard_map/all_gather | solution.py:50
  313.6 10.9 %fusion.4 = f32[320,1280]{1,0:T(8,128)} fusion(f32[1,1280,1280]{2,1,0:T(8,128)} %all-gather.9.cloned.1.call-done, f32[1,320,1280]{2,1,0:T(8,128)S(1)} %copy-done.2, f32[1280]{0:T(1024)S(1)} %get-tuple-element.5), kind=kOutput, calls=%fused_computation.4 | convolution fusion | flops 6291865600 | bytes 9835520 | tf_op jit(solution)/shard_map/cij,cjk->cik/dot_general | solution.py:8
  324.5 6.3 %reduce.5 = f32[320,64,20]{0,2,1:T(8,128)S(1)} reduce(f32[1,320,64,20]{1,0,3,2:T(1,128)} %all-to-all-done.2, f32[]{:T(128)} %constant.18), dimensions={0}, to_apply=%all_to_all.11.reduce_sub_computation | reduce | bytes 3276804 | tf_op jit(solution)/shard_map/all_to_all | solution.py:45
  330.8 1.5 reshape.162
  332.3 2.3 copy.23
  334.6 51.8 %all-gather.7.cloned.1.call-done = f32[1,1280,1280]{2,1,0:T(8,128)} async-done(((f32[1,320,1280]{2,1,0:T(8,128)}), f32[1,1280,1280]{2,1,0:T(8,128)}) %all-gather.7.cloned.1.call-update) | async-done | bytes 6553616 | tf_op jit(solution)/shard_map/all_gather | solution.py:51
  386.4 11.5 %fusion.20 = f32[1,320,1280]{2,1,0:T(8,128)} fusion(f32[320,1280]{1,0:T(8,128)S(1)} %copy.23, f32[320,1280]{1,0:T(8,128)} %fusion.4, f32[1,1280,1280]{2,1,0:T(8,128)} %all-gather.7.cloned.1.call-done, f32[1280]{0:T(1024)S(1)} %fusion.37, f32[320]{0:T(512)S(1)} %fusion.38, f32[1280]{0:T(1024)S(1)} %get-tuple-element.5, f32[1,320,1280]{2,1,0:T(8,128)S(1)} %copy-done.6), kind=kOutput, calls=%fused_computation.15 | convolution fusion | flops 6294323200 | bytes 13118720 | tf_op jit(solution)/shard_map/cij,cjk->cik/dot_general | solution.py:8
  (24 shorter events, 0.1 us)
Async XLA Ops:
  6.5 175.8 %all-gather.11.cloned.1.call-start = ((), (), s32[]{:S(2)}) async-start(), calls=%async_computation.5 | async-start | bytes 8192000 | tf_op jit(solution)/shard_map/all_gather | solution.py:38
  9.4 3.6 copy-start.1
  9.5 85.9 %copy-start.5 = (f32[1,320,1280]{2,1,0:T(8,128)}, f32[1,320,1280]{2,1,0:T(8,128)S(1)}, u32[]{:S(2)}) copy-start(f32[1,320,1280]{2,1,0:T(8,128)S(1)} %get-tuple-element.7) | copy-start | bytes 4915204
  95.3 145.3 %all-gather.13.cloned.1.call-start = ((), (), s32[]{:S(2)}) async-start(), calls=%async_computation.6 | async-start | bytes 8192000 | tf_op jit(solution)/shard_map/all_gather | solution.py:37
  172.5 141.1 %all-gather.9.cloned.1.call-start = ((), (), s32[]{:S(2)}) async-start(), calls=%async_computation.4 | async-start | bytes 8192000 | tf_op jit(solution)/shard_map/all_gather | solution.py:50
  173.2 213.2 %all-gather.7.cloned.1.call-start = ((), (), s32[]{:S(2)}) async-start(), calls=%async_computation.3 | async-start | bytes 8192000 | tf_op jit(solution)/shard_map/all_gather | solution.py:51
  173.8 8.5 %copy-start.7 = (s32[1,1280]{1,0:T(1,128)S(1)}, s32[1,1280]{1,0:T(1,128)}, u32[]{:S(2)}) copy-start(s32[1,1280]{1,0:T(1,128)} %param.11) | copy-start | bytes 15364
  173.8 8.5 %copy-start.8 = (s32[1,1280]{1,0:T(1,128)S(1)}, s32[1,1280]{1,0:T(1,128)}, u32[]{:S(2)}) copy-start(s32[1,1280]{1,0:T(1,128)} %param.10) | copy-start | bytes 15364
  173.8 8.5 %copy-start.4 = (f32[320,1280]{1,0:T(8,128)S(1)}, f32[320,1280]{1,0:T(8,128)}, u32[]{:S(2)}) copy-start(f32[320,1280]{1,0:T(8,128)} %fusion.2) | copy-start | bytes 4915204
  182.4 58.2 %copy-start.3 = (f32[320,1280]{1,0:T(8,128)S(1)}, f32[320,1280]{1,0:T(8,128)}, u32[]{:S(2)}) copy-start(f32[320,1280]{1,0:T(8,128)} %fusion) | copy-start | bytes 4915204
  240.6 10.5 %copy-start = (f32[64,20,1280]{2,1,0:T(8,128)S(1)}, f32[64,20,1280]{2,1,0:T(8,128)}, u32[]{:S(2)}) copy-start(f32[64,20,1280]{2,1,0:T(8,128)} %dot_general.37) | copy-start | bytes 19660804
  266.0 47.6 %copy-start.2 = (f32[1,320,1280]{2,1,0:T(8,128)S(1)}, f32[1,320,1280]{2,1,0:T(8,128)}, u32[]{:S(2)}) copy-start(f32[1,320,1280]{2,1,0:T(8,128)} %copy-done.1) | copy-start | bytes 4915204
  266.0 58.5 %all-to-all-start.2 = ((f32[1,320,64,20]{1,0,3,2:T(1,128)}), f32[1,320,64,20]{1,0,3,2:T(1,128)}, u32[]{:S(2)}, u32[]{:S(2)}) async-start(f32[1,320,64,20]{1,0,3,2:T(1,128)} %copy.22), calls=%async_computation.2 | async-start | bytes 3932160 | tf_op jit(solution)/shard_map/all_to_all | solution.py:45
  332.3 54.2 %copy-start.6 = (f32[1,320,1280]{2,1,0:T(8,128)S(1)}, f32[1,320,1280]{2,1,0:T(8,128)}, u32[]{:S(2)}) copy-start(f32[1,320,1280]{2,1,0:T(8,128)} %param.6) | copy-start | bytes 4915204
Sparse Core Ops, SparseCore 0:
  95.4 67.9 all-gather.10
  172.6 67.9 all-gather.12
  242.4 71.1 all-gather.8
  315.3 71.1 all-gather.6
where the time goes:
time: 411 us; the launch traced here: 405 us
  waiting for transfers between devices  136 us (33%)
  blocking collectives  114 us (28%)
  matrix products  78.5 us (19%)
  local copies, waits for them, and re-layouts  27.1 us (7%)
  other arithmetic  23.3 us (6%)
  between operations  14.4 us (4%)
  starting transfers between devices  11.2 us (3%)
    dot_general x6, matrix products, batched(): jnp.einsum('cij,cjk->cik', left, right, precision=lax.Precision.HIGHEST)  66.9 us
    all_to_all x1, blocking collectives, shards(): lax.all_to_all(ham_live.reshape(piece_shape), 'chan', split_axis=2, conca...  60.2 us
    all_to_all x1, blocking collectives, shards(): lax.all_to_all(gen_live.reshape(piece_shape), 'chan', split_axis=2, conca...  54.1 us
    all_gather x1, waiting for transfers between devices, shards(): lax.all_gather(ham_live, 'row', axis=1, tiled=True)  51.8 us
    all_gather x1, waiting for transfers between devices, shards(): lax.all_gather(gen_bar, 'row', axis=1, tiled=True)  46.6 us
    all_gather x1, waiting for transfers between devices, shards(): lax.all_gather(gen_live, 'row', axis=1, tiled=True)  36.6 us
    dot_general x2, local copies, waits for them, and re-layouts, shards(): jnp.einsum('cij,ckj->cik', ph_term, recoupling, precision=lax.Precision.H...  11.7 us
    dot_general x1, matrix products, shards(): jnp.einsum('cij,ckj->cik', ph_term, recoupling, precision=lax.Precision.H...  11.5 us
  transfers between devices with their start and end apart: 5, of which 3 were waited for; matrix products, arithmetic and copies ran while one was open for 22% of the time, Pallas kernels for 0%

commit v1 on v0

--- a/solution.py
+++ b/solution.py
@@ -1,7 +1,17 @@
+import functools
 import jax
 import jax.numpy as jnp
 from jax import lax
 from jax.sharding import PartitionSpec as P
+
+
+def choose_paths(array_here, mesh_name, d_out, array_dim):
+    view_out = jnp.split(array_here, jax.lax.axis_size(mesh_name), axis=d_out)
+    y = jax.lax.all_to_all(jnp.stack(view_out, axis=0), mesh_name, 0, 0)
+    return jnp.concatenate(y, axis=array_dim)
+
+
+things_connect = functools.partial(choose_paths, mesh_name="chan", d_out=2, array_dim=2)
 
 
 def batched(left, right):
@@ -27,9 +37,7 @@
         lax.all_to_all(
             gen_live.reshape(piece_shape), "chan", split_axis=2, concat_axis=2, tiled=True
         ),
-        lax.all_to_all(
-            ham_live.reshape(piece_shape), "chan", split_axis=2, concat_axis=2, tiled=True
-        ),
+        things_connect(ham_live.reshape(piece_shape)),
     )
     gen_bar = batched(gen_moved.reshape(generator.shape), recoupling)
     ham_bar = batched(ham_moved.reshape(generator.shape), recoupling)

time: 411 us -> 435 us (1.058)
  local copies, waits for them, and re-layouts: 27.1 us -> 48 us
  blocking collectives: 114 us -> 124 us
  other arithmetic: 23.3 us -> 17.8 us
    another operation x2 -> x8, local copies, waits for them, and re-layouts: 4.85 us -> 24.5 us  [the longest x6 18.9 us: choose_paths(): y = jax.lax.all_to_all(jnp.stack(view_out, axis=0), mesh_name, 0, 0)]
    all_to_all x1, blocking collectives: 60.2 us -> 71.3 us  [choose_paths(): y = jax.lax.all_to_all(jnp.stack(view_out, axis=0), mesh_name, 0, 0)]
    all_to_all x1 -> x0, other arithmetic: 7.73 us -> none  [shards(): lax.all_to_all(ham_live.reshape(piece_shape), 'chan', split_axis=2, conca...]
where the time goes in v1:
time: 435 us; the launch traced here: 428 us
  waiting for transfers between devices  133 us (31%)
  blocking collectives  124 us (29%)
  matrix products  79 us (18%)
  local copies, waits for them, and re-layouts  48 us (11%)
  other arithmetic  17.8 us (4%)
  between operations  14.4 us (3%)
  starting transfers between devices  11.2 us (3%)
    all_to_all x1, blocking collectives, choose_paths(): y = jax.lax.all_to_all(jnp.stack(view_out, axis=0), mesh_name, 0, 0)  71.3 us
    dot_general x6, matrix products, batched(): jnp.einsum('cij,cjk->cik', left, right, precision=lax.Precision.HIGHEST)  67.5 us
    all_to_all x1, blocking collectives, shards(): lax.all_to_all(gen_live.reshape(piece_shape), 'chan', split_axis=2, conca...  52.5 us
    all_gather x1, waiting for transfers between devices, shards(): lax.all_gather(ham_live, 'row', axis=1, tiled=True)  49.1 us
    all_gather x1, waiting for transfers between devices, shards(): lax.all_gather(gen_bar, 'row', axis=1, tiled=True)  46.5 us
    all_gather x1, waiting for transfers between devices, shards(): lax.all_gather(gen_live, 'row', axis=1, tiled=True)  36.5 us
    another operation x6, local copies, waits for them, and re-layouts, choose_paths(): y = jax.lax.all_to_all(jnp.stack(view_out, axis=0), mesh_name, 0, 0)  18.9 us
    dot_general x2, local copies, waits for them, and re-layouts, shards(): jnp.einsum('cij,ckj->cik', ph_term, recoupling, precision=lax.Precision.H...  11.8 us
  transfers between devices with their start and end apart: 5, of which 3 were waited for; matrix products, arithmetic and copies ran while one was open for 22% of the time, Pallas kernels for 0%

profile of v1, /device:TPU:1, one launch (start us, length us, event | category | flops | bytes accessed | tf_op | source)
XLA Modules:
  0.0 427.7 jit_solution(13047888640361887224)
XLA Ops:
  7.2 2.2 multiply_multiply_fusion.1
  9.5 3.5 copy.85
  13.0 1.6 slice_bitcast_fusion
  14.6 1.7 slice_bitcast_fusion.19
  16.3 1.7 slice_bitcast_fusion.38
  18.0 1.6 slice_bitcast_fusion.57
  19.6 9.6 %stack.259 = f32[64,1,320,1,20]{2,0,4,3,1:T(8,128)} concatenate(f32[1,1,320,1,20]{2,0,4,3,1:T(1,128)} %get-tuple-element.70, f32[1,1,320,1,20]{2,0,4,3,1:T(1,128)} %get-tuple-element.69, f32[1,1,320,1,20]{2,0,4,3,1:T(1,128)} %get-tuple-element.68, f32[1,1,320,1,20]{2,0,4,3,1:T(1,128)} %get-tuple-element.67, f32[1,1,320,1,20]{2,0,4,3,1:T(1,128)} %get-tuple-element.66, ...), dimensions={0} | concatenate | bytes 3276800 | tf_op jit(solution)/shard_map/stack | solution.py:10
  29.2 2.7 copy.86
  31.9 71.3 %all_to_all.15 = f32[64,1,320,1,20]{2,4,3,1,0:T(8,128)} all-to-all(f32[64,1,320,1,20]{2,4,3,1,0:T(8,128)S(1)} %copy.86), channel_id=1, replica_groups=mesh['chan'=64,'row'=4] {'chan'}, dimensions={0} | all-to-all | bytes 3276800 | tf_op jit(solution)/shard_map/all_to_all | solution.py:10
  103.2 2.7 reshape.162
  105.8 11.5 %fusion = f32[320,1280]{1,0:T(8,128)} fusion(f32[320,1280]{0,1:T(8,128)} %reshape.162, f32[1,1280,1280]{2,1,0:T(8,128)} %param.8), kind=kOutput, calls=%fused_computation | convolution fusion | flops 6291456000 | bytes 9830400 | tf_op jit(solution)/shard_map/cij,cjk->cik/dot_general | solution.py:18
  117.4 3.2 copy.84
  120.6 52.5 %all_to_all.16 = f32[1,320,64,20]{1,0,3,2:T(1,128)} all-to-all(f32[1,320,64,20]{1,0,3,2:T(1,128)} %bitcast.177), channel_id=1, replica_groups=mesh['chan'=64,'row'=4] {'chan'}, dimensions={2} | all-to-all | bytes 3276800 | tf_op jit(solution)/shard_map/all_to_all | solution.py:37
  173.1 7.8 %reduce.2 = f32[320,64,20]{0,2,1:T(8,128)} reduce(f32[1,320,64,20]{1,0,3,2:T(1,128)} %all_to_all.16, f32[]{:T(128)} %constant.18), dimensions={0}, to_apply=%all_to_all.9.reduce_sub_computation | reduce | bytes 3276804 | tf_op jit(solution)/shard_map/all_to_all | solution.py:37
  180.8 2.9 reshape.158
  183.8 11.5 %fusion.2 = f32[320,1280]{1,0:T(8,128)} fusion(f32[320,1280]{0,1:T(8,128)} %reshape.158, f32[1,1280,1280]{2,1,0:T(8,128)} %param.8), kind=kOutput, calls=%fused_computation.2 | convolution fusion | flops 6291456000 | bytes 9830400 | tf_op jit(solution)/shard_map/cij,cjk->cik/dot_general | solution.py:18
  195.3 0.7 all-gather.9.cloned.1.call-update
  196.1 0.5 all-gather.7.cloned.1.call-update
  196.6 8.5 %dot_general.37 = f32[64,20,1280]{2,1,0:T(8,128)} reshape(f32[1,1280,1280]{2,1,0:T(8,128)} %param.8) | data formatting | bytes 13107200 | tf_op jit(solution)/shard_map/cij,ckj->cik/dot_general | solution.py:52
  205.2 11.6 %fusion.26 = f32[320,1280]{1,0:T(8,128)} fusion(f32[1280,1280]{1,0:T(8,128)} %all-gather.11.cloned.1.call-done, f32[320,1280]{1,0:T(8,128)S(1)} %copy-done.4, f32[1280]{0:T(1024)S(1)} %get-tuple-element.6), kind=kOutput, calls=%fused_computation.21 | convolution fusion | flops 6291865600 | bytes 9835520 | tf_op jit(solution)/shard_map/cij,cjk->cik/dot_general | solution.py:18
  216.8 46.5 %all-gather.13.cloned.1.call-done = f32[1280,1280]{1,0:T(8,128)} async-done(((f32[320,1280]{1,0:T(8,128)}), f32[1280,1280]{1,0:T(8,128)}) %all-gather.13.cloned.1.call-update) | async-done | bytes 6553616 | tf_op jit(solution)/shard_map/all_gather | solution.py:45
  263.4 10.5 %fusion.19 = f32[320,1280,1]{1,0,2:T(8,128)S(1)} fusion(f32[320,1280]{1,0:T(8,128)} %fusion.26, f32[1280,1280]{1,0:T(8,128)} %all-gather.13.cloned.1.call-done, f32[320,1280]{1,0:T(8,128)S(1)} %copy-done.3, f32[1280]{0:T(1024)S(1)} %get-tuple-element.6), kind=kOutput, calls=%fused_computation.14 | convolution fusion | flops 6292275200 | bytes 11473920 | tf_op jit(solution)/shard_map/cij,cjk->cik/dot_general | solution.py:18
  273.9 11.5 %fusion.30 = f32[1,320,64,20]{1,2,3,0:T(8,128)S(1)} fusion(f32[320,1280,1]{1,0,2:T(8,128)S(1)} %fusion.19, f32[64,20,1280]{2,1,0:T(8,128)S(1)} %copy-done), kind=kOutput, calls=%fused_computation.25 | convolution fusion | flops 6291456000 | bytes 9830400 | tf_op jit(solution)/shard_map/cij,ckj->cik/dot_general | solution.py:52
  285.4 3.3 copy.88
  288.8 11.0 %all-to-all-start.2 = ((f32[1,320,64,20]{1,0,3,2:T(1,128)}), f32[1,320,64,20]{1,0,3,2:T(1,128)}, u32[]{:S(2)}, u32[]{:S(2)}) async-start(f32[1,320,64,20]{1,0,3,2:T(1,128)} %copy.88), calls=%async_computation.2 | async-start | bytes 3932160 | tf_op jit(solution)/shard_map/all_to_all | solution.py:53
  299.8 36.5 %all-gather.9.cloned.1.call-done = f32[1,1280,1280]{2,1,0:T(8,128)} async-done(((f32[1,320,1280]{2,1,0:T(8,128)}), f32[1,1280,1280]{2,1,0:T(8,128)}) %all-gather.9.cloned.1.call-update) | async-done | bytes 6553616 | tf_op jit(solution)/shard_map/all_gather | solution.py:58
  336.4 10.9 %fusion.4 = f32[320,1280]{1,0:T(8,128)} fusion(f32[1,1280,1280]{2,1,0:T(8,128)} %all-gather.9.cloned.1.call-done, f32[1,320,1280]{2,1,0:T(8,128)S(1)} %copy-done.2, f32[1280]{0:T(1024)S(1)} %get-tuple-element.5), kind=kOutput, calls=%fused_computation.4 | convolution fusion | flops 6291865600 | bytes 9835520 | tf_op jit(solution)/shard_map/cij,cjk->cik/dot_general | solution.py:18
  347.3 7.8 %reduce.4 = f32[320,64,20]{0,2,1:T(8,128)} reduce(f32[1,320,64,20]{1,0,3,2:T(1,128)} %all-to-all-done.2, f32[]{:T(128)} %constant.18), dimensions={0}, to_apply=%all_to_all.11.reduce_sub_computation | reduce | bytes 3276804 | tf_op jit(solution)/shard_map/all_to_all | solution.py:53
  355.0 2.8 reshape.165
  357.9 2.2 copy.89
  360.1 49.1 %all-gather.7.cloned.1.call-done = f32[1,1280,1280]{2,1,0:T(8,128)} async-done(((f32[1,320,1280]{2,1,0:T(8,128)}), f32[1,1280,1280]{2,1,0:T(8,128)}) %all-gather.7.cloned.1.call-update) | async-done | bytes 6553616 | tf_op jit(solution)/shard_map/all_gather | solution.py:59
  409.2 11.5 %fusion.20 = f32[1,320,1280]{2,1,0:T(8,128)} fusion(f32[320,1280]{1,0:T(8,128)S(1)} %copy.89, f32[320,1280]{1,0:T(8,128)} %fusion.4, f32[1,1280,1280]{2,1,0:T(8,128)} %all-gather.7.cloned.1.call-done, f32[1280]{0:T(1024)S(1)} %fusion.37, f32[320]{0:T(512)S(1)} %fusion.38, f32[1280]{0:T(1024)S(1)} %get-tuple-element.5, f32[1,320,1280]{2,1,0:T(8,128)S(1)} %copy-done.6), kind=kOutput, calls=%fused_computation.15 | convolution fusion | flops 6294323200 | bytes 13118720 | tf_op jit(solution)/shard_map/cij,cjk->cik/dot_general | solution.py:18
  (29 shorter events, 0.3 us)
Async XLA Ops:
  6.5 198.6 %all-gather.11.cloned.1.call-start = ((), (), s32[]{:S(2)}) async-start(), calls=%async_computation.5 | async-start | bytes 8192000 | tf_op jit(solution)/shard_map/all_gather | solution.py:46
  9.4 3.5 copy-start.1
  9.5 107.9 %copy-start.5 = (f32[1,320,1280]{2,1,0:T(8,128)}, f32[1,320,1280]{2,1,0:T(8,128)S(1)}, u32[]{:S(2)}) copy-start(f32[1,320,1280]{2,1,0:T(8,128)S(1)} %get-tuple-element.71) | copy-start | bytes 4915204
  117.3 146.0 %all-gather.13.cloned.1.call-start = ((), (), s32[]{:S(2)}) async-start(), calls=%async_computation.6 | async-start | bytes 8192000 | tf_op jit(solution)/shard_map/all_gather | solution.py:45
  195.3 141.1 %all-gather.9.cloned.1.call-start = ((), (), s32[]{:S(2)}) async-start(), calls=%async_computation.4 | async-start | bytes 8192000 | tf_op jit(solution)/shard_map/all_gather | solution.py:58
  196.0 213.2 %all-gather.7.cloned.1.call-start = ((), (), s32[]{:S(2)}) async-start(), calls=%async_computation.3 | async-start | bytes 8192000 | tf_op jit(solution)/shard_map/all_gather | solution.py:59
  196.6 8.5 %copy-start.7 = (s32[1,1280]{1,0:T(1,128)S(1)}, s32[1,1280]{1,0:T(1,128)}, u32[]{:S(2)}) copy-start(s32[1,1280]{1,0:T(1,128)} %param.11) | copy-start | bytes 15364
  196.6 8.5 %copy-start.8 = (s32[1,1280]{1,0:T(1,128)S(1)}, s32[1,1280]{1,0:T(1,128)}, u32[]{:S(2)}) copy-start(s32[1,1280]{1,0:T(1,128)} %param.10) | copy-start | bytes 15364
  196.6 8.6 %copy-start.4 = (f32[320,1280]{1,0:T(8,128)S(1)}, f32[320,1280]{1,0:T(8,128)}, u32[]{:S(2)}) copy-start(f32[320,1280]{1,0:T(8,128)} %fusion.2) | copy-start | bytes 4915204
  205.2 58.2 %copy-start.3 = (f32[320,1280]{1,0:T(8,128)S(1)}, f32[320,1280]{1,0:T(8,128)}, u32[]{:S(2)}) copy-start(f32[320,1280]{1,0:T(8,128)} %fusion) | copy-start | bytes 4915204
  263.4 10.5 %copy-start = (f32[64,20,1280]{2,1,0:T(8,128)S(1)}, f32[64,20,1280]{2,1,0:T(8,128)}, u32[]{:S(2)}) copy-start(f32[64,20,1280]{2,1,0:T(8,128)} %dot_general.37) | copy-start | bytes 19660804
  288.8 47.6 %copy-start.2 = (f32[1,320,1280]{2,1,0:T(8,128)S(1)}, f32[1,320,1280]{2,1,0:T(8,128)}, u32[]{:S(2)}) copy-start(f32[1,320,1280]{2,1,0:T(8,128)} %copy-done.1) | copy-start | bytes 4915204
  288.8 58.5 %all-to-all-start.2 = ((f32[1,320,64,20]{1,0,3,2:T(1,128)}), f32[1,320,64,20]{1,0,3,2:T(1,128)}, u32[]{:S(2)}, u32[]{:S(2)}) async-start(f32[1,320,64,20]{1,0,3,2:T(1,128)} %copy.88), calls=%async_computation.2 | async-start | bytes 3932160 | tf_op jit(solution)/shard_map/all_to_all | solution.py:53
  357.9 51.3 %copy-start.6 = (f32[1,320,1280]{2,1,0:T(8,128)S(1)}, f32[1,320,1280]{2,1,0:T(8,128)}, u32[]{:S(2)}) copy-start(f32[1,320,1280]{2,1,0:T(8,128)} %param.6) | copy-start | bytes 4915204
Sparse Core Ops, SparseCore 0:
  117.4 65.7 all-gather.10
  195.4 67.9 all-gather.12
  265.2 71.1 all-gather.8
  338.0 71.1 all-gather.6
